TPU v7x, 256 devices: a whole 4x4x8 slice. The times are simulated.
256 devices in a mesh: cores: 2 (over core), row: 16 (over y, x), vec: 8 (over z).
Axes of the slice: x: 4, y: 4, z: 8, core: 2. Of those that a mesh axis runs over, the one named last changes fastest.
Arguments:
- train_cores: float32 [8, 512, 256, 256], P('vec', 'cores', 'row'), may hold values from -0.01953125 to 0.01953125
- sketch: float32 [512, 128], P('cores'), may hold values from -6 to 6
- exit_sketch: float32 [256, 128], replicated, may hold values from -6 to 6
Outputs:
- rounded: float32 [8, 256, 256, 128], P('vec', 'cores', 'row')
- interface_bases: float32 [8, 512, 128], P('vec', 'cores')
- margins: float32 [8, 256, 1024], P('vec', 'cores')
All inputs are finite; a program needn't handle non-finite values.
Results may differ from a plain program's by a relative error of at most 0.0003.
Values sent between devices are 32-bit elements; how exact they have to be, the bound alone decides.
A program may use at most 128 MiB of HBM per device.

v0:
```python
import math
import jax
import jax.numpy as jnp
from jax import lax
from jax.sharding import PartitionSpec as P

MODE = 256


def broadcast(block, axis, holder):
    block = jnp.where(lax.axis_index(axis) == holder, block, jnp.zeros_like(block))
    return lax.psum(block, axis)


def product(left_mat, right_mat):
    return jnp.dot(
        left_mat, right_mat, precision=lax.Precision.HIGHEST, preferred_element_type=jnp.float32
    )


def orthonormal(gram_matrix, sketch):
    powered = product(gram_matrix, product(gram_matrix, sketch))
    chol_low = jnp.linalg.cholesky(product(powered.T, powered))
    return jax.scipy.linalg.solve_triangular(chol_low, powered.T, lower=True).T


def local(train_cores, sketch, exit_sketch):
    block_core = train_cores[0]
    full_rank = block_core.shape[0]
    mode_count = block_core.shape[1]
    kept_rank = sketch.shape[1]
    chain_len = lax.axis_size("cores")
    position = lax.axis_index("cores")
    vector_count = lax.axis_size("vec")
    identity = jnp.eye(full_rank, dtype=jnp.float32)
    zero_square = jnp.zeros((full_rank, full_rank), jnp.float32)
    row_major = block_core.reshape(full_rank * mode_count, full_rank)
    wide_core = block_core.reshape(full_rank, mode_count * full_rank)

    def forward_gram(lower_in):
        absorbed = product(lower_in.T, wide_core).reshape(full_rank * mode_count, full_rank)
        return product(absorbed.T, absorbed)

    def zero_gram(operand):
        return zero_square

    lower_prev = identity
    lower_own = identity
    gram_own = identity
    for link_index in range(chain_len):
        active = position == link_index
        partial_value = lax.cond(active, forward_gram, zero_gram, lower_prev)
        summed = jnp.where(active, lax.psum(partial_value, "row"), identity)
        factor = jnp.linalg.cholesky(summed)
        if link_index + 1 < chain_len:
            arrived = broadcast(factor, "cores", link_index)
            lower_prev = jnp.where(position == link_index + 1, arrived, lower_prev)
        lower_own = jnp.where(active, factor, lower_own)
        gram_own = jnp.where(active, summed, gram_own)
    is_last = position == chain_len - 1
    incoming = orthonormal(gram_own, exit_sketch)

    def right_map_of(incoming_frame):
        solved = jax.scipy.linalg.solve_triangular(lower_own, incoming_frame, lower=True, trans=1)
        return jnp.where(is_last, incoming_frame, solved)

    def backward_gram(incoming_frame):
        reduced = product(row_major, right_map_of(incoming_frame)).reshape(
            full_rank, mode_count * kept_rank
        )
        mixed_core = product(lower_prev.T, reduced)
        return product(mixed_core, mixed_core.T)

    frame_own = jnp.zeros((full_rank, kept_rank), jnp.float32)
    for link_index in range(chain_len):
        target = chain_len - 1 - link_index
        active = position == target
        partial_value = lax.cond(active, backward_gram, zero_gram, incoming)
        summed = jnp.where(active, lax.psum(partial_value, "row"), identity)
        frame = orthonormal(summed, sketch)
        if target > 0:
            arrived = broadcast(frame, "cores", target)
            incoming = jnp.where(position == target - 1, arrived, incoming)
        frame_own = jnp.where(active, frame, frame_own)
    reduced = product(row_major, right_map_of(incoming)).reshape(full_rank, mode_count * kept_rank)
    front_map = product(frame_own.T, lower_prev.T)
    shaped = product(front_map, reduced)
    rounded = (shaped * math.sqrt(kept_rank * MODE)).reshape(1, kept_rank, mode_count, kept_rank)
    bases_out = (frame_own * math.sqrt(full_rank))[None]
    gathered, frames_all = (
        lax.all_gather(shaped[None], "vec", axis=0, tiled=True),
        lax.all_gather(frame_own[None], "vec", axis=0, tiled=True),
    )
    start_env = jnp.einsum("az,qay->qzy", frame_own, frames_all, precision=lax.Precision.HIGHEST)
    mine_rows = shaped.reshape(kept_rank * mode_count, kept_rank)
    zero_env = jnp.zeros((vector_count, kept_rank, kept_rank), jnp.float32)

    def margin_terms(env_in):
        carried = jnp.einsum("qzw,qwx->qzx", env_in, gathered, precision=lax.Precision.HIGHEST)
        carried = carried.reshape(vector_count, kept_rank * mode_count, kept_rank)
        return jnp.einsum("cb,qcy->qby", mine_rows, carried, precision=lax.Precision.HIGHEST)

    def zero_margin(operand):
        return zero_env

    env_in = start_env
    env_own = zero_env
    for link_index in range(chain_len):
        active = position == link_index
        partial_value = lax.cond(active, margin_terms, zero_margin, env_in)
        summed = lax.psum(partial_value, "row")
        if link_index + 1 < chain_len:
            arrived = broadcast(summed, "cores", link_index)
            env_in = jnp.where(position == link_index + 1, arrived, env_in)
        env_own = jnp.where(active, summed, env_own)
    margins = env_own.transpose(1, 0, 2).reshape(kept_rank, vector_count * kept_rank)[None]
    return (rounded, bases_out, margins)


def solution(mesh):
    return jax.shard_map(
        local,
        mesh=mesh,
        in_specs=(P("vec", "cores", "row", None), P("cores", None), P()),
        out_specs=(
            P("vec", "cores", "row", None),
            P("vec", "cores", None),
            P("vec", "cores", None),
        ),
        check_vma=False,
    )
```

profile of v0, /device:TPU:1, one launch (start us, length us, event | category | flops | bytes accessed | tf_op | source)
XLA Modules:
  0.0 1188.9 jit_solution(5875113720510303117)
XLA Ops:
  7.3 7.9 copy.89
  16.3 119.6 %all-reduce.11.cloned.1.call-done = f32[256,256]{0,1:T(8,128)} async-done(((f32[256,256]{0,1:T(8,128)}), f32[256,256]{0,1:T(8,128)}) %all-reduce.11.cloned.1.call-update) | async-done | bytes 262160 | tf_op jit(solution)/shard_map/psum | solution.py:53
  136.2 11.7 cholesky.187
  148.0 9.8 custom-call.23
  158.4 11.7 cholesky.204
  173.1 32.5 %all-reduce.13.cloned.1.call-done = f32[256,256]{0,1:T(8,128)} async-done(((f32[256,256]{0,1:T(8,128)}), f32[256,256]{0,1:T(8,128)}) %all-reduce.13.cloned.1.call-update) | async-done | bytes 262160 | tf_op jit(solution)/shard_map/psum | solution.py:12
  205.6 1.0 convert_select_fusion.5
  206.6 23.0 %conditional.7 = (f32[256,256]{1,0:T(8,128)S(1)}) conditional(s32[]{:T(128)} %convert_element_type.28, () %tuple.49, (f32[256,256]{0,1:T(8,128)S(1)}, f32[256,4096]{1,0:T(8,128)}) %tuple.170), branch_computations={%region_8.10_spmd, %region_9.11_spmd} | conditional | flops 6442450944 | bytes 21495816 | solution.py:52
  206.6 8.2 fusion.96
  214.8 4.9 reshape.48
  219.6 9.9 fusion.97
  230.7 93.4 %all-reduce.15.cloned.1.call-done = f32[256,256]{0,1:T(8,128)} async-done(((f32[256,256]{0,1:T(8,128)}), f32[256,256]{0,1:T(8,128)}) %all-reduce.15.cloned.1.call-update) | async-done | bytes 262160 | tf_op jit(solution)/shard_map/psum | solution.py:53
  324.1 1.0 convert_select_fusion.4
  325.2 1.0 fusion.29
  326.2 11.7 cholesky.221
  338.1 9.8 custom-call.24
  348.5 11.7 cholesky.238
  360.4 1.6 fusion.51
  361.9 1.6 fusion.49
  364.0 12.1 %cholesky.253 = f32[128,128]{1,0:T(8,128)S(1)} custom-call(f32[128,128]{1,0:T(8,128)S(1)} %fusion.69), custom_call_target="Cholesky" | custom-call | tf_op jit(solution)/shard_map/jit(cholesky)/cholesky | solution.py:23
  377.4 9.8 custom-call.25
  390.3 42.7 %conditional.8 = (f32[256,256]{1,0:T(8,128)S(1)}) conditional(s32[]{:T(128)} %convert_element_type.28, () %tuple.53, (pred[]{:T(512)}, f32[256,256]{0,1:T(8,128)S(1)}, f32[256,128]{0,1:T(8,128)S(1)}, f32[4096,256]{1,0:T(8,128)}, f32[256,256]{0,1:T(8,128)S(1)}) %tuple.167), branch_computations={%region_13.17_spmd, %region_14.19_spmd} | conditional | flops 4907548672 | bytes 23855310 | solution.py:78
  390.8 3.8 while.6
  391.4 1.3 bitcast_dynamic-update-slice_fusion.8
  393.3 1.3 bitcast_dynamic-update-slice_fusion.8
  394.6 19.7 %custom-call.21 = f32[2,128,128]{1,2,0:T(8,128)S(1)} custom-call(f32[2,128,128]{2,1,0:T(8,128)S(1)} %get-tuple-element.113), custom_call_target="InvertDiagBlocksLowerTriangular" | custom-call | tf_op jit(solution)/shard_map/cond/branch_1_fun/jit(_solve_triangular)/triangular_solve | solution.py:64
  415.0 6.7 convolution_bitcast_fusion.2
  421.7 1.9 copy.42
  423.6 1.9 reshape.49
  425.5 3.6 fusion.99
  429.1 3.6 fusion.100
  433.9 91.5 %all-reduce.17.cloned.1.call-done = f32[256,256]{0,1:T(8,128)} async-done(((f32[256,256]{0,1:T(8,128)}), f32[256,256]{0,1:T(8,128)}) %all-reduce.17.cloned.1.call-update) | async-done | bytes 262160 | tf_op jit(solution)/shard_map/psum | solution.py:79
  525.4 1.5 fusion.35
  526.9 1.6 fusion.34
  529.0 11.7 cholesky.264
  542.1 9.8 custom-call.26
  551.9 1.0 fusion.24
  552.9 28.4 %all-reduce.19.cloned.1.call-done = f32[256,128]{0,1:T(8,128)} async-done(((f32[256,128]{0,1:T(8,128)}), f32[256,128]{0,1:T(8,128)}) %all-reduce.19.cloned.1.call-update) | async-done | bytes 131088 | tf_op jit(solution)/shard_map/psum | solution.py:12
  581.3 6.4 conditional.9
  588.6 131.1 %all-reduce.21.cloned.1.call-done = f32[256,256]{0,1:T(8,128)} async-done(((f32[256,256]{0,1:T(8,128)}), f32[256,256]{0,1:T(8,128)}) %all-reduce.21.cloned.1.call-update) | async-done | bytes 262160 | tf_op jit(solution)/shard_map/psum | solution.py:79
  721.5 11.7 cholesky.275
  734.5 9.8 custom-call.27
  745.7 4.0 while.8
  746.3 1.3 dynamic-slice.19
  748.3 1.3 dynamic-slice.19
  749.7 19.7 %custom-call.28 = f32[2,128,128]{1,2,0:T(8,128)S(1)} custom-call(f32[2,128,128]{2,1,0:T(8,128)S(1)} %get-tuple-element.115), custom_call_target="InvertDiagBlocksLowerTriangular" | custom-call | tf_op jit(solution)/shard_map/jit(_solve_triangular)/triangular_solve | solution.py:64
  770.3 6.5 convolution_bitcast_fusion.4
  776.8 1.9 copy.69
  778.7 1.7 reshape.56
  780.7 2.2 fusion.107
  783.0 1.4 reshape.58
  784.4 2.2 convolution_bitcast_fusion.5
  786.7 95.5 %all-gather.7.cloned.1.call-done = f32[1024,2048]{1,0:T(8,128)} async-done(((f32[128,2048]{1,0:T(8,128)}), f32[1024,2048]{1,0:T(8,128)}) %all-gather.7.cloned.1.call-update) | async-done | bytes 8388624 | tf_op jit(solution)/shard_map/all_gather | solution.py:91
  883.5 129.1 %all-reduce.23.cloned.1.call-done = f32[8,128,128]{1,2,0:T(8,128)} async-done(((f32[8,128,128]{1,2,0:T(8,128)}), f32[8,128,128]{1,2,0:T(8,128)}) %all-reduce.23.cloned.1.call-update) | async-done | bytes 524304 | tf_op jit(solution)/shard_map/psum | solution.py:111
  1013.5 33.1 %all-reduce.25.cloned.1.call-done = f32[8,128,128]{1,2,0:T(8,128)} async-done(((f32[8,128,128]{1,2,0:T(8,128)}), f32[8,128,128]{1,2,0:T(8,128)}) %all-reduce.25.cloned.1.call-update) | async-done | bytes 524304 | tf_op jit(solution)/shard_map/psum | solution.py:12
  1046.6 38.8 %conditional.11 = (f32[8,128,128]{1,2,0:T(8,128)}) conditional(s32[]{:T(128)} %convert_element_type.28, () %tuple.56, (pred[]{:T(512)}, f32[8,128,128]{1,2,0:T(8,128)}, f32[8,128,128]{1,2,0:T(8,128)S(1)}, f32[8,128,2048]{2,1,0:T(8,128)}, f32[2048,128]{1,0:T(8,128)S(1)}) %tuple.172), branch_computations={%region_24.29_spmd, %region_25.30_spmd} | conditional | flops 6442582016 | bytes 46661640 | solution.py:110
  1047.0 1.2 copy.73
  1048.2 11.7 fusion.2
  1059.9 9.3 reshape.52
  1069.2 16.2 %convolution_bitcast_fusion.1 = f32[8,128,128]{1,2,0:T(8,128)} fusion(f32[8,2048,128]{2,1,0:T(8,128)} %reshape.52, f32[2048,128]{1,0:T(8,128)S(1)} %get-tuple-element.89), kind=kOutput, calls=%fused_computation.2 | convolution fusion | flops 3221225472 | bytes 9961472 | tf_op jit(solution)/shard_map/cond/branch_1_fun/cb,qcy->qby/dot_general | solution.py:101
  1086.3 1.2 copy.90
  1087.4 92.6 %all-reduce.27.cloned.1.call-done = f32[8,128,128]{1,2,0:T(8,128)} async-done(((f32[8,128,128]{1,2,0:T(8,128)}), f32[8,128,128]{1,2,0:T(8,128)}) %all-reduce.27.cloned.1.call-update) | async-done | bytes 524304 | tf_op jit(solution)/shard_map/psum | solution.py:111
  1180.1 1.1 broadcast_select_fusion.1
  1181.2 1.0 copy.86
  (139 shorter events, 25.5 us)
Async XLA Ops:
  7.2 518.2 %copy-start = (f32[256,128]{1,0:T(8,128)S(1)}, f32[256,128]{1,0:T(8,128)}, u32[]{:S(2)}) copy-start(f32[256,128]{1,0:T(8,128)} %param.22) | copy-start | bytes 393220
  7.2 128.7 %all-reduce.11.cloned.1.call-start = ((), (), s32[]{:S(2)}) async-start(), calls=%async_computation | async-start | bytes 524288 | tf_op jit(solution)/shard_map/psum | solution.py:53
  16.1 189.5 %all-reduce.13.cloned.1.call-start = ((), (), s32[]{:S(2)}) async-start(), calls=%async_computation.1 | async-start | bytes 524288 | tf_op jit(solution)/shard_map/psum | solution.py:12
  173.0 151.1 %all-reduce.15.cloned.1.call-start = ((), (), s32[]{:S(2)}) async-start(), calls=%async_computation.2 | async-start | bytes 524288 | tf_op jit(solution)/shard_map/psum | solution.py:53
  206.5 153.8 %copy-start.3 = (f32[256,256]{0,1:T(8,128)S(1)}, f32[256,256]{0,1:T(8,128)}, u32[]{:S(2)}) copy-start(f32[256,256]{0,1:T(8,128)} %all-reduce.11.cloned.1.call-done) | copy-start | bytes 786436
  206.6 153.8 %copy-start.8 = (f32[256,128]{1,0:T(8,128)S(1)}, f32[256,128]{1,0:T(8,128)}, u32[]{:S(2)}) copy-start(f32[256,128]{1,0:T(8,128)} %param.23) | copy-start | bytes 393220
  230.4 295.0 %all-reduce.17.cloned.1.call-start = ((), (), s32[]{:S(2)}) async-start(), calls=%async_computation.3 | async-start | bytes 524288 | tf_op jit(solution)/shard_map/psum | solution.py:79
  433.8 147.4 %all-reduce.19.cloned.1.call-start = ((), (), s32[]{:S(2)}) async-start(), calls=%async_computation.4 | async-start | bytes 262144 | tf_op jit(solution)/shard_map/psum | solution.py:12
  552.9 166.9 %all-reduce.21.cloned.1.call-start = ((), (), s32[]{:S(2)}) async-start(), calls=%async_computation.5 | async-start | bytes 524288 | tf_op jit(solution)/shard_map/psum | solution.py:79
  581.3 163.0 %copy-start.7 = (f32[256,128]{0,1:T(8,128)S(1)}, f32[256,128]{0,1:T(8,128)}, u32[]{:S(2)}) copy-start(f32[256,128]{0,1:T(8,128)} %fusion.24) | copy-start | bytes 393220
  588.6 195.9 %all-gather.5.cloned.1.call-start = ((), (), s32[]{:S(2)}) async-start(), calls=%async_computation.9 | async-start | bytes 1179648 | tf_op jit(solution)/shard_map/all_gather | solution.py:92
  745.3 136.8 %all-gather.7.cloned.1.call-start = ((), (), s32[]{:S(2)}) async-start(), calls=%async_computation.10 | async-start | bytes 9437184 | tf_op jit(solution)/shard_map/all_gather | solution.py:91
  776.8 3.6 copy-start.4
  783.0 229.6 %all-reduce.23.cloned.1.call-start = ((), (), s32[]{:S(2)}) async-start(), calls=%async_computation.6 | async-start | bytes 1048576 | tf_op jit(solution)/shard_map/psum | solution.py:111
  882.6 0.8 copy-start.5
  883.4 163.2 %all-reduce.25.cloned.1.call-start = ((), (), s32[]{:S(2)}) async-start(), calls=%async_computation.7 | async-start | bytes 1048576 | tf_op jit(solution)/shard_map/psum | solution.py:12
  1013.4 166.6 %all-reduce.27.cloned.1.call-start = ((), (), s32[]{:S(2)}) async-start(), calls=%async_computation.8 | async-start | bytes 1048576 | tf_op jit(solution)/shard_map/psum | solution.py:111
  1046.6 39.6 %copy-start.2 = (f32[128,2048]{1,0:T(8,128)S(1)}, f32[128,2048]{1,0:T(8,128)}, u32[]{:S(2)}) copy-start(f32[128,2048]{1,0:T(8,128)} %fusion.107) | copy-start | bytes 3145732
  1085.4 94.7 %copy-start.6 = (f32[8,128,128]{1,2,0:T(8,128)S(1)}, f32[8,128,128]{1,2,0:T(8,128)}, u32[]{:S(2)}) copy-start(f32[8,128,128]{1,2,0:T(8,128)} %all-reduce.23.cloned.1.call-done) | copy-start | bytes 1572868
  1085.4 96.8 %copy-start.1 = (f32[256,128]{1,0:T(8,128)S(1)}, f32[256,128]{1,0:T(8,128)}, u32[]{:S(2)}) copy-start(f32[256,128]{1,0:T(8,128)} %param.22) | copy-start | bytes 393220
Sparse Core Ops, SparseCore 0:
  16.2 119.6 all-reduce.10
  173.2 32.3 all-reduce.12
  230.5 93.5 all-reduce.14
  434.0 91.3 all-reduce.16
  553.0 28.2 all-reduce.18
  588.7 131.0 all-reduce.20
  745.5 37.0 all-gather.4
  785.1 96.9 all-gather.6
  886.2 126.2 all-reduce.22
  1015.6 30.9 all-reduce.24
  1085.5 94.4 all-reduce.26
where the time goes:
time: 1200 us; the launch traced here: 1190 us
  waiting for transfers between devices  847 us (71%)
  other arithmetic  183 us (15%)
  matrix products  84.3 us (7%)
  local copies, waits for them, and re-layouts  48.8 us (4%)
  between operations  17.2 us (1%)
    psum x4, waiting for transfers between devices, local(): summed = jnp.where(active, lax.psum(partial_value, 'row'), identity)  436 us
    psum x2, waiting for transfers between devices, local(): summed = lax.psum(partial_value, 'row')  222 us
    all_gather x1, waiting for transfers between devices, local(): lax.all_gather(shaped[None], 'vec', axis=0, tiled=True)  95.5 us
    psum x3, waiting for transfers between devices, broadcast(): return lax.psum(block, axis)  94 us
    another operation x13, other arithmetic, local(): factor = jnp.linalg.cholesky(summed)  68.5 us
    dot_general x17, matrix products, product(): jnp.dot(left_mat, right_mat, precision=lax.Precision.HIGHEST, preferred_e...  49.5 us
    another operation x8, other arithmetic, right_map_of(): jax.scipy.linalg.solve_triangular(lower_own, incoming_frame, lower=True,...  39.4 us
    another operation x9, other arithmetic, orthonormal(): chol_low = jnp.linalg.cholesky(product(powered.T, powered))  37.6 us
  transfers between devices with their start and end apart: 11, of which 10 were waited for; matrix products, arithmetic and copies ran while one was open for 4% of the time, Pallas kernels for 0%

commit v1 on v0

--- a/solution.py
+++ b/solution.py
@@ -108,7 +108,9 @@
     for link_index in range(chain_len):
         active = position == link_index
         partial_value = lax.cond(active, margin_terms, zero_margin, env_in)
-        summed = lax.psum(partial_value, "row")
+        summed = partial_value
+        for hop in (1, 2, 4, 8):
+            summed = summed + lax.ppermute(summed, "row", [(dev, dev ^ hop) for dev in range(16)])
         if link_index + 1 < chain_len:
             arrived = broadcast(summed, "cores", link_index)
             env_in = jnp.where(position == link_index + 1, arrived, env_in)

time: 1200 us -> 1080 us (0.900)
  waiting for transfers between devices: 847 us -> 707 us
  starting transfers between devices: 1.05 us -> 25.6 us
    psum x2 -> x0, waiting for transfers between devices: 222 us -> none  [local(): summed = lax.psum(partial_value, 'row')]
    ppermute x0 -> x8, waiting for transfers between devices: none -> 53.6 us  [local(): lax.ppermute(summed, 'row', [(dev, dev ^ hop) for dev in range(16)])]
    psum x3, waiting for transfers between devices: 94 us -> 131 us  [broadcast(): return lax.psum(block, axis)]
    ppermute x0 -> x8, starting transfers between devices: none -> 15.8 us  [local(): lax.ppermute(summed, 'row', [(dev, dev ^ hop) for dev in range(16)])]
  transfers between devices with their start and end apart: 11 -> 17, of which waited for: 10 -> 16; matrix products, arithmetic and copies ran while one was open for 4% -> 4% of each run, Pallas kernels for 0% -> 0%
where the time goes in v1:
time: 1080 us; the launch traced here: 1070 us
  waiting for transfers between devices  707 us (65%)
  other arithmetic  182 us (17%)
  matrix products  83.6 us (8%)
  local copies, waits for them, and re-layouts  48.7 us (5%)
  starting transfers between devices  25.6 us (2%)
  between operations  17.5 us (2%)
    psum x4, waiting for transfers between devices, local(): summed = jnp.where(active, lax.psum(partial_value, 'row'), identity)  427 us
    psum x3, waiting for transfers between devices, broadcast(): return lax.psum(block, axis)  131 us
    all_gather x1, waiting for transfers between devices, local(): lax.all_gather(shaped[None], 'vec', axis=0, tiled=True)  94.9 us
    another operation x13, other arithmetic, local(): factor = jnp.linalg.cholesky(summed)  68.5 us
    ppermute x8, waiting for transfers between devices, local(): lax.ppermute(summed, 'row', [(dev, dev ^ hop) for dev in range(16)])  53.6 us
    dot_general x17, matrix products, product(): jnp.dot(left_mat, right_mat, precision=lax.Precision.HIGHEST, preferred_e...  49.4 us
    another operation x8, other arithmetic, right_map_of(): jax.scipy.linalg.solve_triangular(lower_own, incoming_frame, lower=True,...  39.4 us
    another operation x9, other arithmetic, orthonormal(): chol_low = jnp.linalg.cholesky(product(powered.T, powered))  37.4 us
  transfers between devices with their start and end apart: 17, of which 16 were waited for; matrix products, arithmetic and copies ran while one was open for 4% of the time, Pallas kernels for 0%

profile of v1, /device:TPU:1, one launch (start us, length us, event | category | flops | bytes accessed | tf_op | source)
XLA Modules:
  0.0 1071.3 jit_solution(12912831958783108902)
XLA Ops:
  7.3 7.9 copy.89
  16.4 119.5 %all-reduce.9.cloned.1.call-done = f32[256,256]{0,1:T(8,128)} async-done(((f32[256,256]{0,1:T(8,128)}), f32[256,256]{0,1:T(8,128)}) %all-reduce.9.cloned.1.call-update) | async-done | bytes 262160 | tf_op jit(solution)/shard_map/psum | solution.py:53
  136.2 11.7 %cholesky.187 = f32[128,128]{1,0:T(8,128)S(1)} custom-call(f32[128,128]{1,0:T(8,128)S(1)} %cholesky.284), custom_call_target="Cholesky" | custom-call | tf_op jit(solution)/shard_map/jit(cholesky)/cholesky | solution.py:54
  148.0 9.8 custom-call.23
  158.4 11.7 %cholesky.204 = f32[128,128]{1,0:T(8,128)S(1)} custom-call(f32[128,128]{1,0:T(8,128)S(1)} %convolution_subtract_fusion.4), custom_call_target="Cholesky" | custom-call | tf_op jit(solution)/shard_map/jit(cholesky)/cholesky | solution.py:54
  173.1 32.5 %all-reduce.11.cloned.1.call-done = f32[256,256]{0,1:T(8,128)} async-done(((f32[256,256]{0,1:T(8,128)}), f32[256,256]{0,1:T(8,128)}) %all-reduce.11.cloned.1.call-update) | async-done | bytes 262160 | tf_op jit(solution)/shard_map/psum | solution.py:12
  206.6 23.0 %conditional.7 = (f32[256,256]{1,0:T(8,128)S(1)}) conditional(s32[]{:T(128)} %convert_element_type.28, () %tuple.49, (f32[256,256]{0,1:T(8,128)S(1)}, f32[256,4096]{1,0:T(8,128)}) %tuple.166), branch_computations={%region_8.10_spmd, %region_9.11_spmd} | conditional | flops 6442450944 | bytes 21495816 | solution.py:52
  206.6 8.2 fusion.96
  214.8 4.9 reshape.48
  219.7 9.9 fusion.97
  230.4 8.8 all-reduce.15.cloned.1.call-start
  239.2 84.9 %all-reduce.13.cloned.1.call-done = f32[256,256]{0,1:T(8,128)} async-done(((f32[256,256]{0,1:T(8,128)}), f32[256,256]{0,1:T(8,128)}) %all-reduce.13.cloned.1.call-update) | async-done | bytes 262160 | tf_op jit(solution)/shard_map/psum | solution.py:53
  326.3 11.7 %cholesky.221 = f32[128,128]{1,0:T(8,128)S(1)} custom-call(f32[128,128]{1,0:T(8,128)S(1)} %cholesky.287), custom_call_target="Cholesky" | custom-call | tf_op jit(solution)/shard_map/jit(cholesky)/cholesky | solution.py:54
  338.1 9.8 custom-call.24
  348.5 11.7 %cholesky.238 = f32[128,128]{1,0:T(8,128)S(1)} custom-call(f32[128,128]{1,0:T(8,128)S(1)} %convolution_subtract_fusion.3), custom_call_target="Cholesky" | custom-call | tf_op jit(solution)/shard_map/jit(cholesky)/cholesky | solution.py:54
  360.4 1.6 fusion.51
  362.0 1.6 fusion.49
  364.0 11.9 %cholesky.253 = f32[128,128]{1,0:T(8,128)S(1)} custom-call(f32[128,128]{1,0:T(8,128)S(1)} %fusion.69), custom_call_target="Cholesky" | custom-call | tf_op jit(solution)/shard_map/jit(cholesky)/cholesky | solution.py:23
  377.3 9.8 custom-call.25
  390.1 43.2 %conditional.8 = (f32[256,256]{1,0:T(8,128)S(1)}) conditional(s32[]{:T(128)} %convert_element_type.28, () %tuple.53, (pred[]{:T(512)}, f32[256,256]{0,1:T(8,128)S(1)}, f32[256,128]{0,1:T(8,128)S(1)}, f32[4096,256]{1,0:T(8,128)}, f32[256,256]{0,1:T(8,128)S(1)}) %tuple.163), branch_computations={%region_13.17_spmd, %region_14.19_spmd} | conditional | flops 4907548672 | bytes 23855310 | solution.py:78
  390.7 4.1 while.6
  393.4 1.4 bitcast_dynamic-update-slice_fusion.8
  394.8 19.7 %custom-call.21 = f32[2,128,128]{1,2,0:T(8,128)S(1)} custom-call(f32[2,128,128]{2,1,0:T(8,128)S(1)} %get-tuple-element.113), custom_call_target="InvertDiagBlocksLowerTriangular" | custom-call | tf_op jit(solution)/shard_map/cond/branch_1_fun/jit(_solve_triangular)/triangular_solve | solution.py:64
  415.2 6.7 convolution_bitcast_fusion.2
  421.9 1.9 copy.42
  423.7 2.2 reshape.49
  425.9 3.6 fusion.99
  429.5 3.6 fusion.100
  434.2 91.5 %all-reduce.15.cloned.1.call-done = f32[256,256]{0,1:T(8,128)} async-done(((f32[256,256]{0,1:T(8,128)}), f32[256,256]{0,1:T(8,128)}) %all-reduce.15.cloned.1.call-update) | async-done | bytes 262160 | tf_op jit(solution)/shard_map/psum | solution.py:79
  525.7 1.5 fusion.35
  527.3 1.6 fusion.34
  529.3 11.7 %cholesky.264 = f32[128,128]{1,0:T(8,128)S(1)} custom-call(f32[128,128]{1,0:T(8,128)S(1)} %fusion.67), custom_call_target="Cholesky" | custom-call | tf_op jit(solution)/shard_map/jit(cholesky)/cholesky | solution.py:23
  542.4 9.8 custom-call.26
  553.2 28.4 %all-reduce.17.cloned.1.call-done = f32[256,128]{0,1:T(8,128)} async-done(((f32[256,128]{0,1:T(8,128)}), f32[256,128]{0,1:T(8,128)}) %all-reduce.17.cloned.1.call-update) | async-done | bytes 131088 | tf_op jit(solution)/shard_map/psum | solution.py:12
  581.6 6.2 conditional.9
  588.8 131.2 %all-reduce.19.cloned.1.call-done = f32[256,256]{0,1:T(8,128)} async-done(((f32[256,256]{0,1:T(8,128)}), f32[256,256]{0,1:T(8,128)}) %all-reduce.19.cloned.1.call-update) | async-done | bytes 262160 | tf_op jit(solution)/shard_map/psum | solution.py:79
  721.7 11.7 %cholesky.275 = f32[128,128]{1,0:T(8,128)S(1)} custom-call(f32[128,128]{1,0:T(8,128)S(1)} %fusion.65), custom_call_target="Cholesky" | custom-call | tf_op jit(solution)/shard_map/jit(cholesky)/cholesky | solution.py:23
  734.8 9.8 custom-call.27
  746.2 4.3 while.8
  750.5 19.7 %custom-call.28 = f32[2,128,128]{1,2,0:T(8,128)S(1)} custom-call(f32[2,128,128]{2,1,0:T(8,128)S(1)} %get-tuple-element.115), custom_call_target="InvertDiagBlocksLowerTriangular" | custom-call | tf_op jit(solution)/shard_map/jit(_solve_triangular)/triangular_solve | solution.py:64
  771.1 6.5 convolution_bitcast_fusion.4
  777.6 1.9 copy.69
  779.4 1.7 reshape.56
  781.4 2.2 fusion.107
  785.1 2.2 convolution_bitcast_fusion.5
  787.4 94.9 %all-gather.7.cloned.1.call-done = f32[1024,2048]{1,0:T(8,128)} async-done(((f32[128,2048]{1,0:T(8,128)}), f32[1024,2048]{1,0:T(8,128)}) %all-gather.7.cloned.1.call-update) | async-done | bytes 8388624 | tf_op jit(solution)/shard_map/all_gather | solution.py:91
  883.8 6.8 collective-permute-done
  890.7 2.8 collective-permute-start.1
  893.5 6.8 collective-permute-done.1
  900.4 1.5 collective-permute-start.2
  901.9 6.8 collective-permute-done.2
  908.8 2.8 collective-permute-start.3
  911.6 6.8 collective-permute-done.3
  919.3 70.0 %all-reduce.21.cloned.1.call-done = f32[8,128,128]{1,2,0:T(8,128)} async-done(((f32[8,128,128]{1,2,0:T(8,128)}), f32[8,128,128]{1,2,0:T(8,128)}) %all-reduce.21.cloned.1.call-update) | async-done | bytes 524304 | tf_op jit(solution)/shard_map/psum | solution.py:12
  989.4 37.9 %conditional.11 = (f32[8,128,128]{1,2,0:T(8,128)S(1)}) conditional(s32[]{:T(128)} %convert_element_type.28, () %tuple.56, (pred[]{:T(512)}, f32[8,128,128]{1,2,0:T(8,128)}, f32[8,128,128]{1,2,0:T(8,128)S(1)}, f32[8,128,2048]{2,1,0:T(8,128)}, f32[2048,128]{1,0:T(8,128)S(1)}) %tuple.168), branch_computations={%region_23.28_spmd, %region_24.29_spmd} | conditional | flops 6442582016 | bytes 46661640 | solution.py:110
  990.8 11.7 %fusion.2 = f32[8,128,2048]{2,1,0:T(8,128)} fusion(f32[8,128,2048]{2,1,0:T(8,128)} %get-tuple-element.88, f32[8,128,128]{2,1,0:T(8,128)S(1)} %copy.73, f32[8,128,128]{2,1,0:T(8,128)S(1)} %copy.74, pred[]{:T(512)} %get-tuple-element.85), kind=kOutput, calls=%fused_computation.4 | convolution fusion | flops 3221356544 | bytes 17825792 | tf_op jit(solution)/shard_map/cond/branch_1_fun/qzw,qwx->qzx/dot_general | solution.py:99
  1002.5 9.3 reshape.52
  1011.7 15.5 %convolution_bitcast_fusion.1 = f32[8,128,128]{1,2,0:T(8,128)S(1)} fusion(f32[8,2048,128]{2,1,0:T(8,128)} %reshape.52, f32[2048,128]{1,0:T(8,128)S(1)} %get-tuple-element.89), kind=kOutput, calls=%fused_computation.2 | convolution fusion | flops 3221225472 | bytes 9961472 | tf_op jit(solution)/shard_map/cond/branch_1_fun/cb,qcy->qby/dot_general | solution.py:101
  1028.6 7.1 collective-permute-done.4
  1035.7 2.5 collective-permute-start.5
  1038.3 7.1 collective-permute-done.5
  1046.5 7.1 collective-permute-done.6
  1053.6 2.6 collective-permute-start.7
  1058.2 5.0 collective-permute-done.7
  (153 shorter events, 41.5 us)
Async XLA Ops:
  7.2 518.6 %copy-start = (f32[256,128]{1,0:T(8,128)S(1)}, f32[256,128]{1,0:T(8,128)}, u32[]{:S(2)}) copy-start(f32[256,128]{1,0:T(8,128)} %param.22) | copy-start | bytes 393220
  7.2 128.7 %all-reduce.9.cloned.1.call-start = ((), (), s32[]{:S(2)}) async-start(), calls=%async_computation | async-start | bytes 524288 | tf_op jit(solution)/shard_map/psum | solution.py:53
  16.1 189.5 %all-reduce.11.cloned.1.call-start = ((), (), s32[]{:S(2)}) async-start(), calls=%async_computation.1 | async-start | bytes 524288 | tf_op jit(solution)/shard_map/psum | solution.py:12
  173.0 151.1 %all-reduce.13.cloned.1.call-start = ((), (), s32[]{:S(2)}) async-start(), calls=%async_computation.2 | async-start | bytes 524288 | tf_op jit(solution)/shard_map/psum | solution.py:53
  206.5 153.8 %copy-start.4 = (f32[256,256]{0,1:T(8,128)S(1)}, f32[256,256]{0,1:T(8,128)}, u32[]{:S(2)}) copy-start(f32[256,256]{0,1:T(8,128)} %all-reduce.9.cloned.1.call-done) | copy-start | bytes 786436
  206.6 153.8 %copy-start.7 = (f32[256,128]{1,0:T(8,128)S(1)}, f32[256,128]{1,0:T(8,128)}, u32[]{:S(2)}) copy-start(f32[256,128]{1,0:T(8,128)} %param.23) | copy-start | bytes 393220
  230.4 295.3 %all-reduce.15.cloned.1.call-start = ((), (), s32[]{:S(2)}) async-start(), calls=%async_computation.3 | async-start | bytes 524288 | tf_op jit(solution)/shard_map/psum | solution.py:79
  434.1 147.5 %all-reduce.17.cloned.1.call-start = ((), (), s32[]{:S(2)}) async-start(), calls=%async_computation.4 | async-start | bytes 262144 | tf_op jit(solution)/shard_map/psum | solution.py:12
  553.2 166.8 %all-reduce.19.cloned.1.call-start = ((), (), s32[]{:S(2)}) async-start(), calls=%async_computation.5 | async-start | bytes 524288 | tf_op jit(solution)/shard_map/psum | solution.py:79
  581.6 162.9 %copy-start.6 = (f32[256,128]{0,1:T(8,128)S(1)}, f32[256,128]{0,1:T(8,128)}, u32[]{:S(2)}) copy-start(f32[256,128]{0,1:T(8,128)} %fusion.24) | copy-start | bytes 393220
  588.7 196.4 %all-gather.5.cloned.1.call-start = ((), (), s32[]{:S(2)}) async-start(), calls=%async_computation.7 | async-start | bytes 1179648 | tf_op jit(solution)/shard_map/all_gather | solution.py:92
  745.6 136.7 %all-gather.7.cloned.1.call-start = ((), (), s32[]{:S(2)}) async-start(), calls=%async_computation.8 | async-start | bytes 9437184 | tf_op jit(solution)/shard_map/all_gather | solution.py:91
  777.5 3.6 copy-start.5
  783.7 205.7 %all-reduce.21.cloned.1.call-start = ((), (), s32[]{:S(2)}) async-start(), calls=%async_computation.6 | async-start | bytes 1048576 | tf_op jit(solution)/shard_map/psum | solution.py:12
  882.5 8.1 collective-permute-start
  890.7 9.6 collective-permute-start.1
  900.4 8.3 collective-permute-start.2
  908.8 9.6 collective-permute-start.3
  1027.3 29.7 %copy-start.2 = (f32[128,2048]{1,0:T(8,128)S(1)}, f32[128,2048]{1,0:T(8,128)}, u32[]{:S(2)}) copy-start(f32[128,2048]{1,0:T(8,128)} %fusion.107) | copy-start | bytes 3145732
  1027.3 8.4 collective-permute-start.4
  1035.7 27.5 %copy-start.3 = (f32[8,128,128]{1,2,0:T(8,128)S(1)}, f32[8,128,128]{1,2,0:T(8,128)}, u32[]{:S(2)}) copy-start(f32[8,128,128]{1,2,0:T(8,128)} %add_select_fusion.1) | copy-start | bytes 1572868
  1035.7 9.6 collective-permute-start.5
  1045.4 8.1 collective-permute-start.6
  1053.6 10.8 %copy-start.1 = (f32[256,128]{1,0:T(8,128)S(1)}, f32[256,128]{1,0:T(8,128)}, u32[]{:S(2)}) copy-start(f32[256,128]{1,0:T(8,128)} %param.22) | copy-start | bytes 393220
  1053.6 9.6 collective-permute-start.7
Sparse Core Ops, SparseCore 0:
  16.2 119.6 all-reduce.8
  173.2 32.3 all-reduce.10
  230.5 93.5 all-reduce.12
  434.3 91.3 all-reduce.14
  553.3 28.2 all-reduce.16
  588.8 131.1 all-reduce.18
  745.7 36.5 all-gather.4
  784.8 97.4 all-gather.6
  919.5 69.8 all-reduce.20
